TPU v7x, 512 devices: a whole 4x4x16 slice. The times are simulated.
512 devices in a mesh: rows: 32 (over z_lo, y, core), gz: 16 (over z_hi, x).
Axes of the slice: x: 4, y: 4, z: 16 (z_hi: 4, z_lo: 4; z = z_hi * 4 + z_lo), core: 2. Of those that a mesh axis runs over, the one named last changes fastest.
Arguments:
- plane_colour_samples: int32 [32, 3, 1024, 2048], P('gz', None, 'rows'), may hold values from 0 to 255
- clarity_gain: float32 [32], P('gz'), may hold values from 0.01 to 4
Outputs:
- joined: float32 [3, 1024, 2048], P(None, 'rows')
All inputs are finite; a program needn't handle non-finite values.
Results may differ from a plain program's by a relative error of at most 0.000067.
Values sent between devices are 32-bit elements; how exact they have to be, the bound alone decides.
No kernel may reach another device: no remote copies, remote signals or barrier semaphores. Data moves between devices by JAX's collectives and lax.ppermute only.
A program may use at most 64 MiB of HBM per device.

v0:
```python
import jax
import jax.numpy as jnp
from jax import lax
from jax.sharding import PartitionSpec as P


def extended(block, sides, width):
    for axis, dim in sides:
        count = lax.axis_size(axis)
        forward = [(i, i + 1) for i in range(count - 1)]
        backward = [(target, source) for source, target in forward]
        low = lax.ppermute(
            lax.slice_in_dim(block, block.shape[dim] - width, None, axis=dim), axis, forward
        )
        high = lax.ppermute(lax.slice_in_dim(block, 0, width, axis=dim), axis, backward)
        block = jnp.concatenate([low, block, high], axis=dim)
    return block


def blur_rows(padded_image, count):
    return (
        padded_image[..., 0:count, :]
        + 4.0 * padded_image[..., 1 : count + 1, :]
        + 6.0 * padded_image[..., 2 : count + 2, :]
        + 4.0 * padded_image[..., 3 : count + 3, :]
        + padded_image[..., 4 : count + 4, :]
    ) / 16.0


def blur_cols(field):
    count = field.shape[-1]
    padded_image = jnp.pad(field, [(0, 0)] * (field.ndim - 1) + [(2, 2)])
    return (
        padded_image[..., 0:count]
        + 4.0 * padded_image[..., 1 : count + 1]
        + 6.0 * padded_image[..., 2 : count + 2]
        + 4.0 * padded_image[..., 3 : count + 3]
        + padded_image[..., 4 : count + 4]
    ) / 16.0


def upsampled_rows(padded_image, count):
    even = (
        padded_image[..., 0:count, :]
        + 6.0 * padded_image[..., 1 : count + 1, :]
        + padded_image[..., 2 : count + 2, :]
    ) / 8.0
    odd = (padded_image[..., 1 : count + 1, :] + padded_image[..., 2 : count + 2, :]) / 2.0
    shape = even.shape[:-2] + (2 * count, even.shape[-1])
    return jnp.stack([even, odd], axis=-2).reshape(shape)


def up_cols(field):
    count = field.shape[-1]
    padded_image = jnp.pad(field, [(0, 0)] * (field.ndim - 1) + [(1, 1)])
    even = (
        padded_image[..., 0:count]
        + 6.0 * padded_image[..., 1 : count + 1]
        + padded_image[..., 2 : count + 2]
    ) / 8.0
    odd = (padded_image[..., 1 : count + 1] + padded_image[..., 2 : count + 2]) / 2.0
    shape = field.shape[:-1] + (2 * count,)
    return jnp.stack([even, odd], axis=-1).reshape(shape)


def reduce_level(padded_image, count):
    return blur_cols(blur_rows(padded_image, count))[..., ::2, ::2]


def expand_level(padded_image, count):
    return up_cols(upsampled_rows(padded_image, count))


def octave_border(field):
    return extended(field, (("rows", 2),), 2)


def collapse(mixed_finest_band, mixed_coarse_band, blend2, strip):
    central_rows = mixed_coarse_band + expand_level(octave_border(blend2)[..., 1:-1, :], strip // 4)
    return mixed_finest_band + expand_level(octave_border(central_rows)[..., 1:-1, :], strip // 2)


def on_device(plane_colour_samples, clarity_gain):
    strip = plane_colour_samples.shape[2]
    image = plane_colour_samples.astype(jnp.float32) / 255.0
    padded_image = extended(image, (("rows", 2),), 5)
    grey = 0.299 * padded_image[:, 0] + 0.587 * padded_image[:, 1] + 0.114 * padded_image[:, 2]
    side = jnp.pad(grey, ((0, 0), (0, 0), (1, 1)))
    lap = (
        4.0 * grey[:, 1:-1, :]
        - grey[:, :-2, :]
        - grey[:, 2:, :]
        - side[:, 1:-1, :-2]
        - side[:, 1:-1, 2:]
    )
    height = strip * lax.axis_size("rows")
    first_row = lax.axis_index("rows") * strip - 4
    line_slice_from = first_row + jnp.arange(strip + 8, dtype=jnp.int32)
    inside = ((line_slice_from >= 0) & (line_slice_from < height)).astype(jnp.float32)
    squared = lap * lap * inside[None, :, None]
    summed = squared[:, 0:strip]
    for shift in range(1, 9):
        summed = summed + squared[:, shift : shift + strip]
    width = summed.shape[2]
    cols_pad = jnp.pad(summed, ((0, 0), (0, 0), (4, 4)))
    sharpness_measure_field = cols_pad[:, :, 0:width]
    for shift in range(1, 9):
        sharpness_measure_field = sharpness_measure_field + cols_pad[:, :, shift : shift + width]
    clarity_ratings = clarity_gain[:, None, None] * sharpness_measure_field
    top = lax.pmax(jnp.max(clarity_ratings, axis=0), "gz")
    expo = jnp.exp(clarity_ratings - top[None])
    total = lax.psum(jnp.sum(expo, axis=0), "gz")
    weight0 = (expo / total[None])[:, None]
    level1 = reduce_level(padded_image[..., 3:-3, :], strip)
    level1_pad = octave_border(level1)
    level2 = reduce_level(level1_pad, strip // 2)
    padded_level_second = octave_border(level2)
    detail0 = image - expand_level(level1_pad[..., 1:-1, :], strip // 2)
    detail1 = level1 - expand_level(padded_level_second[..., 1:-1, :], strip // 4)
    weight1 = reduce_level(octave_border(weight0), strip)
    weight_level2 = reduce_level(octave_border(weight1), strip // 2)
    mixed_finest_band = jnp.sum(weight0 * detail0, axis=0, keepdims=True)
    mixed_coarse_band = jnp.sum(weight1 * detail1, axis=0, keepdims=True)
    blend2 = jnp.sum(weight_level2 * level2, axis=0, keepdims=True)
    mixed_finest_band, mixed_coarse_band, blend2 = lax.psum(
        (mixed_finest_band, mixed_coarse_band, blend2), "gz"
    )
    joined = collapse(mixed_finest_band, mixed_coarse_band, blend2, strip)
    return joined[0]


def solution(mesh):
    placed = (P("gz", None, "rows", None), P("gz"))
    return jax.shard_map(
        on_device, mesh=mesh, in_specs=placed, out_specs=P(None, "rows", None), check_vma=False
    )
```

profile of v0, /device:TPU:1, one launch (start us, length us, event | category | flops | bytes accessed | tf_op | source)
XLA Modules:
  0.0 865.2 jit_solution(9867116555211420040)
XLA Ops:
  8.4 8.8 %collective-permute-start.1 = (f32[2,3,5,2048]{3,0,2,1:T(2,128)S(1)}, f32[2,3,5,2048]{3,0,2,1:T(2,128)S(1)}, u32[]{:S(2)}, u32[]{:S(2)}) collective-permute-start(f32[2,3,5,2048]{3,0,2,1:T(2,128)S(1)} %copy.379), channel_id=1, source_target_pairs={{16,0},{32,16},{48,32},{64,48},{80,64},{96,80},{112,96},{128,112},... | collective-permute-start | bytes 737288 | tf_op jit(solution)/shard_map/ppermute | solution.py:15
  19.5 2.9 collective-permute-done
  28.5 17.7 %slice.380 = f32[2,3,16,1024]{3,2,1,0:T(8,128)S(1)} slice(f32[2,3,32,2048]{3,2,1,0:T(8,128)S(1)} %add_multiply_fusion), slice={[0:2:1], [0:3:1], [0:32:2], [0:2048:2]} | slice | bytes 786432 | tf_op jit(solution)/shard_map/slice | solution.py:67
  46.3 4.4 collective-permute-start.2
  52.6 4.9 fusion.74
  59.4 4.3 slice.404
  64.3 3.6 collective-permute-start.6
  71.5 181.4 %all-reduce.15.cloned.1.call-done = f32[32,2048]{1,0:T(8,128)} async-done(((f32[32,2048]{1,0:T(8,128)}), f32[32,2048]{1,0:T(8,128)}) %all-reduce.15.cloned.1.call-update) | async-done | bytes 262160 | tf_op jit(solution)/shard_map/pmax | solution.py:110
  254.8 2.5 multiply_bitcast_fusion.2
  259.2 9.2 %copy.387 = f32[2,3,32,1024,2]{2,4,3,1,0:T(2,128)} copy(f32[2,3,32,1024,2]{3,0,2,1,4:T(2,128)} %pad_maximum_fusion.3) | data formatting | bytes 3145728 | tf_op jit(solution)/shard_map/stack | solution.py:63
  268.4 5.6 copy.388
  274.0 183.3 %all-reduce.17.cloned.1.call-done = f32[32,2048]{1,0:T(8,128)} async-done(((f32[32,2048]{1,0:T(8,128)}), f32[32,2048]{1,0:T(8,128)}) %all-reduce.17.cloned.1.call-update) | async-done | bytes 262160 | tf_op jit(solution)/shard_map/psum | solution.py:112
  458.5 14.3 %collective-permute-start.4 = (f32[2,1,2,2048]{3,2,1,0:T(2,128)S(1)}, f32[2,1,2,2048]{3,2,1,0:T(2,128)S(1)}, u32[]{:S(2)}, u32[]{:S(2)}) collective-permute-start(f32[2,1,2,2048]{3,2,1,0:T(2,128)S(1)} %get-tuple-element.25), channel_id=1, source_target_pairs={{0,16},{16,32},{32,48},{48,64},{64,80},{80,96},{96,112},{112,128},... | collective-permute-start | bytes 98312 | tf_op jit(solution)/shard_map/ppermute | solution.py:12
  479.8 6.0 slice.397
  488.7 2.5 collective-permute-start.9
  497.6 110.6 %psum.31 = f32[1,3,8,512]{2,3,1,0:T(8,128)} all-reduce(f32[1,3,8,512]{2,3,1,0:T(8,128)S(1)} %bitcast.84), channel_id=1, replica_groups=mesh['rows'=32,'gz'=16] {'gz'}, use_global_device_ids=true, to_apply=%region_9.10 | all-reduce | flops 12288 | bytes 98304 | tf_op jit(solution)/shard_map/psum | solution.py:125
  609.2 3.5 copy.396
  617.0 12.2 %collective-permute-start.10 = (f32[1,3,2,512]{3,2,1,0:T(2,128)S(1)}, f32[1,3,2,512]{3,2,1,0:T(2,128)S(1)}, u32[]{:S(2)}, u32[]{:S(2)}) collective-permute-start(f32[1,3,2,512]{3,2,1,0:T(2,128)S(1)} %copy.407), channel_id=1, source_target_pairs={{0,16},{16,32},{32,48},{48,64},{64,80},{80,96},{96,112},{112,128},... | collective-permute-start | bytes 36872 | tf_op jit(solution)/shard_map/ppermute | solution.py:12
  631.9 2.5 collective-permute-done.11
  638.2 188.5 %all-reduce.19.cloned.1.call-done = (f32[1,3,32,2048]{3,2,1,0:T(8,128)}, f32[1,3,16,1024]{3,2,1,0:T(8,128)}) async-done(((f32[1,3,32,2048]{3,2,1,0:T(8,128)}, f32[1,3,16,1024]{3,2,1,0:T(8,128)}), (f32[1,3,32,2048]{3,2,1,0:T(8,128)}, f32[1,3,16,1024]{3,2,1,0:T(8,128)})) %all-reduce.19.cloned.1.call-update) | async-done | bytes 983056 | tf_op jit(solution)/shard_map/psum | solution.py:125
  827.7 13.3 %collective-permute-start.12 = (f32[1,3,2,1024]{3,2,1,0:T(2,128)S(1)}, f32[1,3,2,1024]{3,2,1,0:T(2,128)S(1)}, u32[]{:S(2)}, u32[]{:S(2)}) collective-permute-start(f32[1,3,2,1024]{3,2,1,0:T(2,128)S(1)} %get-tuple-element.35), channel_id=1, source_target_pairs={{0,16},{16,32},{32,48},{48,64},{64,80},{80,96},{96,112},{112,128},... | collective-permute-start | bytes 73736 | tf_op jit(solution)/shard_map/ppermute | solution.py:12
  842.9 3.2 collective-permute-done.13
  846.6 2.5 multiply_bitcast_fusion.4
  850.8 3.7 copy.417
  (101 shorter events, 60.1 us)
Async XLA Ops:
  6.5 246.4 %all-reduce.15.cloned.1.call-start = ((), (), s32[]{:S(2)}) async-start(), calls=%async_computation | async-start | bytes 524288 | tf_op jit(solution)/shard_map/pmax | solution.py:110
  8.4 10.9 %collective-permute-start.1 = (f32[2,3,5,2048]{3,0,2,1:T(2,128)S(1)}, f32[2,3,5,2048]{3,0,2,1:T(2,128)S(1)}, u32[]{:S(2)}, u32[]{:S(2)}) collective-permute-start(f32[2,3,5,2048]{3,0,2,1:T(2,128)S(1)} %copy.379), channel_id=1, source_target_pairs={{16,0},{32,16},{48,32},{64,48},{80,64},{96,80},{112,96},{128,112},... | collective-permute-start | bytes 737288 | tf_op jit(solution)/shard_map/ppermute | solution.py:15
  17.4 5.0 collective-permute-start
  26.8 25.8 %copy-start.8 = (f32[2]{0:T(128)S(1)}, f32[2]{0:T(128)}, u32[]{:S(2)}) copy-start(f32[2]{0:T(128)} %param.3) | copy-start | bytes 28
  46.3 11.5 %collective-permute-start.2 = (f32[2,3,2,1024]{3,2,1,0:T(2,128)S(1)}, f32[2,3,2,1024]{3,2,1,0:T(2,128)S(1)}, u32[]{:S(2)}, u32[]{:S(2)}) collective-permute-start(f32[2,3,2,1024]{3,2,1,0:T(2,128)S(1)} %get-tuple-element.31), channel_id=1, source_target_pairs={{0,16},{16,32},{32,48},{48,64},{64,80},{80,96},{96,112},{112,128},... | collective-permute-start | bytes 147464 | tf_op jit(solution)/shard_map/ppermute | solution.py:12
  50.7 7.1 collective-permute-start.3
  57.5 399.8 %all-reduce.17.cloned.1.call-start = ((), (), s32[]{:S(2)}) async-start(), calls=%async_computation.1 | async-start | bytes 524288 | tf_op jit(solution)/shard_map/psum | solution.py:112
  63.7 7.8 copy-start.7
  64.3 431.0 %collective-permute-start.6 = (f32[2,3,2,512]{3,2,1,0:T(2,128)}, f32[2,3,2,512]{3,2,1,0:T(2,128)}, u32[]{:S(2)}, u32[]{:S(2)}) collective-permute-start(f32[2,3,2,512]{3,2,1,0:T(2,128)} %get-tuple-element.46), channel_id=1, source_target_pairs={{0,16},{16,32},{32,48},{48,64},{64,80},{80,96},{96,112},{112,128},... | collective-permute-start | bytes 73736 | tf_op jit(solution)/shard_map/ppermute | solution.py:12
  68.0 427.4 %collective-permute-start.7 = (f32[2,3,2,512]{3,2,1,0:T(2,128)}, f32[2,3,2,512]{3,2,1,0:T(2,128)}, u32[]{:S(2)}, u32[]{:S(2)}) collective-permute-start(f32[2,3,2,512]{3,2,1,0:T(2,128)} %get-tuple-element.47), channel_id=1, source_target_pairs={{16,0},{32,16},{48,32},{64,48},{80,64},{96,80},{112,96},{128,112},... | collective-permute-start | bytes 73736 | tf_op jit(solution)/shard_map/ppermute | solution.py:15
  71.5 183.3 %copy-start.4 = (f32[2,3,16,2,1024]{4,0,3,2,1:T(2,128)S(1)}, f32[2,3,16,2,1024]{4,0,3,2,1:T(2,128)}, u32[]{:S(2)}) copy-start(f32[2,3,16,2,1024]{4,0,3,2,1:T(2,128)} %copy.384) | copy-start | bytes 2359300
  254.7 572.0 %all-reduce.19.cloned.1.call-start = ((), (), s32[]{:S(2)}) async-start(), calls=%async_computation.2 | async-start | bytes 1966080 | tf_op jit(solution)/shard_map/psum | solution.py:125
  268.4 188.9 %copy-start.3 = (f32[32,2048]{1,0:T(8,128)S(1)}, f32[32,2048]{1,0:T(8,128)}, u32[]{:S(2)}) copy-start(f32[32,2048]{1,0:T(8,128)} %all-reduce.15.cloned.1.call-done) | copy-start | bytes 786436
  457.3 17.6 %copy-start.5 = (f32[32,2048]{1,0:T(8,128)S(1)}, f32[32,2048]{1,0:T(8,128)}, u32[]{:S(2)}) copy-start(f32[32,2048]{1,0:T(8,128)} %all-reduce.17.cloned.1.call-done) | copy-start | bytes 786436
  458.5 17.4 %collective-permute-start.4 = (f32[2,1,2,2048]{3,2,1,0:T(2,128)S(1)}, f32[2,1,2,2048]{3,2,1,0:T(2,128)S(1)}, u32[]{:S(2)}, u32[]{:S(2)}) collective-permute-start(f32[2,1,2,2048]{3,2,1,0:T(2,128)S(1)} %get-tuple-element.25), channel_id=1, source_target_pairs={{0,16},{16,32},{32,48},{48,64},{64,80},{80,96},{96,112},{112,128},... | collective-permute-start | bytes 98312 | tf_op jit(solution)/shard_map/ppermute | solution.py:12
  472.8 5.2 collective-permute-start.5
  478.4 12.8 %copy-start.2 = (f32[2,3,32,2048]{3,2,1,0:T(8,128)S(1)}, f32[2,3,32,2048]{3,2,1,0:T(8,128)}, u32[]{:S(2)}) copy-start(f32[2,3,32,2048]{3,2,1,0:T(8,128)} %copy.388) | copy-start | bytes 4718596
  486.8 6.9 collective-permute-start.8
  488.7 5.2 copy-start.6
  488.7 5.2 collective-permute-start.9
  617.0 14.6 %collective-permute-start.10 = (f32[1,3,2,512]{3,2,1,0:T(2,128)S(1)}, f32[1,3,2,512]{3,2,1,0:T(2,128)S(1)}, u32[]{:S(2)}, u32[]{:S(2)}) collective-permute-start(f32[1,3,2,512]{3,2,1,0:T(2,128)S(1)} %copy.407), channel_id=1, source_target_pairs={{0,16},{16,32},{32,48},{48,64},{64,80},{80,96},{96,112},{112,128},... | collective-permute-start | bytes 36872 | tf_op jit(solution)/shard_map/ppermute | solution.py:12
  629.4 5.0 collective-permute-start.11
  827.7 15.2 %collective-permute-start.12 = (f32[1,3,2,1024]{3,2,1,0:T(2,128)S(1)}, f32[1,3,2,1024]{3,2,1,0:T(2,128)S(1)}, u32[]{:S(2)}, u32[]{:S(2)}) collective-permute-start(f32[1,3,2,1024]{3,2,1,0:T(2,128)S(1)} %get-tuple-element.35), channel_id=1, source_target_pairs={{0,16},{16,32},{32,48},{48,64},{64,80},{80,96},{96,112},{112,128},... | collective-permute-start | bytes 73736 | tf_op jit(solution)/shard_map/ppermute | solution.py:12
  840.9 5.1 collective-permute-start.13
  (2 other events, 3.3 us)
Sparse Core Ops, SparseCore 0:
  57.7 195.2 all-reduce.14
  256.1 201.1 all-reduce.16
  616.5 210.0 all-reduce.18
where the time goes:
time: 867 us; the launch traced here: 865 us
  waiting for transfers between devices  564 us (65%)
  blocking collectives  111 us (13%)
  starting transfers between devices  73.2 us (8%)
  local copies, waits for them, and re-layouts  63.7 us (7%)
  other arithmetic  39.8 us (5%)
  between operations  13.6 us (2%)
    psum x1, waiting for transfers between devices, on_device(): lax.psum((mixed_finest_band, mixed_coarse_band, blend2), 'gz')  188 us
    psum x1, waiting for transfers between devices, on_device(): total = lax.psum(jnp.sum(expo, axis=0), 'gz')  183 us
    pmax x1, waiting for transfers between devices, on_device(): top = lax.pmax(jnp.max(clarity_ratings, axis=0), 'gz')  181 us
    psum x1, blocking collectives, on_device(): lax.psum((mixed_finest_band, mixed_coarse_band, blend2), 'gz')  111 us
    ppermute x7, starting transfers between devices, extended(): lax.ppermute(lax.slice_in_dim(block, block.shape[dim] - width, None, axis...  51.6 us
    slice x4, local copies, waits for them, and re-layouts, reduce_level(): return blur_cols(blur_rows(padded_image, count))[..., ::2, ::2]  29.2 us
    ppermute x7, starting transfers between devices, extended(): lax.ppermute(lax.slice_in_dim(block, 0, width, axis=dim), axis, backward)  21.4 us
  transfers between devices with their start and end apart: 17, of which 8 were waited for; matrix products, arithmetic and copies ran while one was open for 6% of the time, Pallas kernels for 0%

commit v1 on v0

--- a/solution.py
+++ b/solution.py
@@ -109,7 +109,7 @@
     clarity_ratings = clarity_gain[:, None, None] * sharpness_measure_field
     top = lax.pmax(jnp.max(clarity_ratings, axis=0), "gz")
     expo = jnp.exp(clarity_ratings - top[None])
-    total = lax.psum(jnp.sum(expo, axis=0), "gz")
+    total = jnp.sum(lax.all_gather(jnp.sum(expo, axis=0), "gz"), axis=0)
     weight0 = (expo / total[None])[:, None]
     level1 = reduce_level(padded_image[..., 3:-3, :], strip)
     level1_pad = octave_border(level1)

time: 867 us -> 761 us (0.88)
  waiting for transfers between devices: 564 us -> 476 us
  blocking collectives: 111 us -> 99 us
    psum x1 -> x0, waiting for transfers between devices: 183 us -> none  [on_device(): total = lax.psum(jnp.sum(expo, axis=0), 'gz')]
    all_gather x0 -> x1, waiting for transfers between devices: none -> 78.2 us  [on_device(): total = jnp.sum(lax.all_gather(jnp.sum(expo, axis=0), 'gz'), axis=0)]
    pmax x1, waiting for transfers between devices: 181 us -> 194 us  [on_device(): top = lax.pmax(jnp.max(clarity_ratings, axis=0), 'gz')]
    psum x1, blocking collectives: 111 us -> 99 us  [on_device(): lax.psum((mixed_finest_band, mixed_coarse_band, blend2), 'gz')]
  transfers between devices with their start and end apart: 17 -> 17, of which waited for: 8 -> 9; matrix products, arithmetic and copies ran while one was open for 6% -> 8% of each run, Pallas kernels for 0% -> 0%
where the time goes in v1:
time: 761 us; the launch traced here: 760 us
  waiting for transfers between devices  476 us (63%)
  blocking collectives  99 us (13%)
  starting transfers between devices  75.2 us (10%)
  local copies, waits for them, and re-layouts  59.2 us (8%)
  other arithmetic  37.5 us (5%)
  between operations  13.7 us (2%)
    pmax x1, waiting for transfers between devices, on_device(): top = lax.pmax(jnp.max(clarity_ratings, axis=0), 'gz')  194 us
    psum x1, waiting for transfers between devices, on_device(): lax.psum((mixed_finest_band, mixed_coarse_band, blend2), 'gz')  190 us
    psum x1, blocking collectives, on_device(): lax.psum((mixed_finest_band, mixed_coarse_band, blend2), 'gz')  99 us
    all_gather x1, waiting for transfers between devices, on_device(): total = jnp.sum(lax.all_gather(jnp.sum(expo, axis=0), 'gz'), axis=0)  78.2 us
    ppermute x7, starting transfers between devices, extended(): lax.ppermute(lax.slice_in_dim(block, block.shape[dim] - width, None, axis...  51.7 us
    slice x4, local copies, waits for them, and re-layouts, reduce_level(): return blur_cols(blur_rows(padded_image, count))[..., ::2, ::2]  28.4 us
    ppermute x7, starting transfers between devices, extended(): lax.ppermute(lax.slice_in_dim(block, 0, width, axis=dim), axis, backward)  23.4 us
  transfers between devices with their start and end apart: 17, of which 9 were waited for; matrix products, arithmetic and copies ran while one was open for 8% of the time, Pallas kernels for 0%

profile of v1, /device:TPU:1, one launch (start us, length us, event | category | flops | bytes accessed | tf_op | source)
XLA Modules:
  0.0 760.3 jit_solution(455375325038389405)
XLA Ops:
  8.4 8.8 %collective-permute-start.1 = (f32[2,3,5,2048]{3,0,2,1:T(2,128)S(1)}, f32[2,3,5,2048]{3,0,2,1:T(2,128)S(1)}, u32[]{:S(2)}, u32[]{:S(2)}) collective-permute-start(f32[2,3,5,2048]{3,0,2,1:T(2,128)S(1)} %copy.435), channel_id=1, source_target_pairs={{16,0},{32,16},{48,32},{64,48},{80,64},{96,80},{112,96},{128,112},... | collective-permute-start | bytes 737288 | tf_op jit(solution)/shard_map/ppermute | solution.py:15
  19.5 2.9 collective-permute-done
  24.9 2.7 fusion.74
  27.7 193.8 %all-reduce.14.cloned.1.call-done = f32[32,2048]{1,0:T(8,128)} async-done(((f32[32,2048]{1,0:T(8,128)}), f32[32,2048]{1,0:T(8,128)}) %all-reduce.14.cloned.1.call-update) | async-done | bytes 262160 | tf_op jit(solution)/shard_map/pmax | solution.py:110
  227.4 17.7 %slice.380 = f32[2,3,16,1024]{3,2,1,0:T(8,128)S(1)} slice(f32[2,3,32,2048]{3,2,1,0:T(8,128)S(1)} %add_multiply_fusion), slice={[0:2:1], [0:3:1], [0:32:2], [0:2048:2]} | slice | bytes 786432 | tf_op jit(solution)/shard_map/slice | solution.py:67
  245.1 14.3 %collective-permute-start.2 = (f32[2,3,2,1024]{3,2,1,0:T(2,128)S(1)}, f32[2,3,2,1024]{3,2,1,0:T(2,128)S(1)}, u32[]{:S(2)}, u32[]{:S(2)}) collective-permute-start(f32[2,3,2,1024]{3,2,1,0:T(2,128)S(1)} %get-tuple-element.31), channel_id=1, source_target_pairs={{0,16},{16,32},{32,48},{48,64},{64,80},{80,96},{96,112},{112,128},... | collective-permute-start | bytes 147464 | tf_op jit(solution)/shard_map/ppermute | solution.py:12
  261.6 3.7 collective-permute-done.3
  266.1 3.4 slice.404
  272.1 3.0 collective-permute-start.7
  275.8 2.5 multiply_bitcast_fusion.2
  279.1 6.5 copy.445
  285.6 5.5 copy.446
  291.1 78.2 %all-gather.3.cloned.1.call-done = f32[512,2048]{1,0:T(8,128)} async-done(((f32[32,2048]{1,0:T(8,128)}), f32[512,2048]{1,0:T(8,128)}) %all-gather.3.cloned.1.call-update) | async-done | bytes 4194320 | tf_op jit(solution)/shard_map/all_gather | solution.py:112
  371.9 4.3 collective-permute-start.4
  383.3 6.0 slice.397
  392.2 2.5 collective-permute-start.9
  401.1 99.0 %psum.23 = f32[1,3,8,512]{2,3,1,0:T(8,128)} all-reduce(f32[1,3,8,512]{2,3,1,0:T(8,128)S(1)} %bitcast.86), channel_id=1, replica_groups=mesh['rows'=32,'gz'=16] {'gz'}, use_global_device_ids=true, to_apply=%region_9.10 | all-reduce | flops 12288 | bytes 98304 | tf_op jit(solution)/shard_map/psum | solution.py:125
  501.1 3.5 copy.454
  508.8 14.1 %collective-permute-start.10 = (f32[1,3,2,512]{3,2,1,0:T(2,128)S(1)}, f32[1,3,2,512]{3,2,1,0:T(2,128)S(1)}, u32[]{:S(2)}, u32[]{:S(2)}) collective-permute-start(f32[1,3,2,512]{3,2,1,0:T(2,128)S(1)} %copy.465), channel_id=1, source_target_pairs={{0,16},{16,32},{32,48},{48,64},{64,80},{80,96},{96,112},{112,128},... | collective-permute-start | bytes 36872 | tf_op jit(solution)/shard_map/ppermute | solution.py:12
  523.2 2.9 collective-permute-start.11
  532.1 189.7 %all-reduce.16.cloned.1.call-done = (f32[1,3,32,2048]{3,2,1,0:T(8,128)}, f32[1,3,16,1024]{3,2,1,0:T(8,128)}) async-done(((f32[1,3,32,2048]{3,2,1,0:T(8,128)}, f32[1,3,16,1024]{3,2,1,0:T(8,128)}), (f32[1,3,32,2048]{3,2,1,0:T(8,128)}, f32[1,3,16,1024]{3,2,1,0:T(8,128)})) %all-reduce.16.cloned.1.call-update) | async-done | bytes 983056 | tf_op jit(solution)/shard_map/psum | solution.py:125
  722.7 13.3 %collective-permute-start.12 = (f32[1,3,2,1024]{3,2,1,0:T(2,128)S(1)}, f32[1,3,2,1024]{3,2,1,0:T(2,128)S(1)}, u32[]{:S(2)}, u32[]{:S(2)}) collective-permute-start(f32[1,3,2,1024]{3,2,1,0:T(2,128)S(1)} %get-tuple-element.35), channel_id=1, source_target_pairs={{0,16},{16,32},{32,48},{48,64},{64,80},{80,96},{96,112},{112,128},... | collective-permute-start | bytes 73736 | tf_op jit(solution)/shard_map/ppermute | solution.py:12
  737.9 3.2 collective-permute-done.13
  745.8 3.7 copy.475
  (102 shorter events, 61.3 us)
Async XLA Ops:
  6.5 215.0 %all-reduce.14.cloned.1.call-start = ((), (), s32[]{:S(2)}) async-start(), calls=%async_computation | async-start | bytes 524288 | tf_op jit(solution)/shard_map/pmax | solution.py:110
  8.4 10.9 %collective-permute-start.1 = (f32[2,3,5,2048]{3,0,2,1:T(2,128)S(1)}, f32[2,3,5,2048]{3,0,2,1:T(2,128)S(1)}, u32[]{:S(2)}, u32[]{:S(2)}) collective-permute-start(f32[2,3,5,2048]{3,0,2,1:T(2,128)S(1)} %copy.435), channel_id=1, source_target_pairs={{16,0},{32,16},{48,32},{64,48},{80,64},{96,80},{112,96},{128,112},... | collective-permute-start | bytes 737288 | tf_op jit(solution)/shard_map/ppermute | solution.py:15
  17.4 5.0 collective-permute-start
  24.9 198.6 %copy-start = (s32[2,3,32,2048]{3,2,1,0:T(8,128)S(1)}, s32[2,3,32,2048]{3,2,1,0:T(8,128)}, u32[]{:S(2)}) copy-start(s32[2,3,32,2048]{3,2,1,0:T(8,128)} %param.2) | copy-start | bytes 4718596
  27.6 341.6 %all-gather.3.cloned.1.call-start = ((), (), s32[]{:S(2)}) async-start(), calls=%async_computation.1 | async-start | bytes 4456448 | tf_op jit(solution)/shard_map/all_gather | solution.py:112
  223.5 498.3 %all-reduce.16.cloned.1.call-start = ((), (), s32[]{:S(2)}) async-start(), calls=%async_computation.2 | async-start | bytes 1966080 | tf_op jit(solution)/shard_map/psum | solution.py:125
  245.1 16.4 %collective-permute-start.2 = (f32[2,3,2,1024]{3,2,1,0:T(2,128)S(1)}, f32[2,3,2,1024]{3,2,1,0:T(2,128)S(1)}, u32[]{:S(2)}, u32[]{:S(2)}) collective-permute-start(f32[2,3,2,1024]{3,2,1,0:T(2,128)S(1)} %get-tuple-element.31), channel_id=1, source_target_pairs={{0,16},{16,32},{32,48},{48,64},{64,80},{80,96},{96,112},{112,128},... | collective-permute-start | bytes 147464 | tf_op jit(solution)/shard_map/ppermute | solution.py:12
  259.4 5.8 collective-permute-start.3
  269.5 6.3 copy-start.7
  270.2 128.6 %collective-permute-start.6 = (f32[2,3,2,512]{3,2,1,0:T(2,128)}, f32[2,3,2,512]{3,2,1,0:T(2,128)}, u32[]{:S(2)}, u32[]{:S(2)}) collective-permute-start(f32[2,3,2,512]{3,2,1,0:T(2,128)} %get-tuple-element.46), channel_id=1, source_target_pairs={{0,16},{16,32},{32,48},{48,64},{64,80},{80,96},{96,112},{112,128},... | collective-permute-start | bytes 73736 | tf_op jit(solution)/shard_map/ppermute | solution.py:12
  272.1 126.7 %collective-permute-start.7 = (f32[2,3,2,512]{3,2,1,0:T(2,128)}, f32[2,3,2,512]{3,2,1,0:T(2,128)}, u32[]{:S(2)}, u32[]{:S(2)}) collective-permute-start(f32[2,3,2,512]{3,2,1,0:T(2,128)} %get-tuple-element.47), channel_id=1, source_target_pairs={{16,0},{32,16},{48,32},{64,48},{80,64},{96,80},{112,96},{128,112},... | collective-permute-start | bytes 73736 | tf_op jit(solution)/shard_map/ppermute | solution.py:15
  369.3 2.5 copy-start.1
  369.3 2.5 copy-start.4
  371.9 7.4 collective-permute-start.4
  376.3 5.2 collective-permute-start.5
  381.9 12.8 %copy-start.3 = (f32[2,3,32,2048]{3,2,1,0:T(8,128)S(1)}, f32[2,3,32,2048]{3,2,1,0:T(8,128)}, u32[]{:S(2)}) copy-start(f32[2,3,32,2048]{3,2,1,0:T(8,128)} %copy.446) | copy-start | bytes 4718596
  390.2 6.9 collective-permute-start.8
  392.2 5.2 copy-start.6
  392.2 5.2 collective-permute-start.9
  506.4 1.9 copy-start.2
  508.8 17.3 %collective-permute-start.10 = (f32[1,3,2,512]{3,2,1,0:T(2,128)S(1)}, f32[1,3,2,512]{3,2,1,0:T(2,128)S(1)}, u32[]{:S(2)}, u32[]{:S(2)}) collective-permute-start(f32[1,3,2,512]{3,2,1,0:T(2,128)S(1)} %copy.465), channel_id=1, source_target_pairs={{0,16},{16,32},{32,48},{48,64},{64,80},{80,96},{96,112},{112,128},... | collective-permute-start | bytes 36872 | tf_op jit(solution)/shard_map/ppermute | solution.py:12
  523.2 5.0 collective-permute-start.11
  722.7 15.2 %collective-permute-start.12 = (f32[1,3,2,1024]{3,2,1,0:T(2,128)S(1)}, f32[1,3,2,1024]{3,2,1,0:T(2,128)S(1)}, u32[]{:S(2)}, u32[]{:S(2)}) collective-permute-start(f32[1,3,2,1024]{3,2,1,0:T(2,128)S(1)} %get-tuple-element.35), channel_id=1, source_target_pairs={{0,16},{16,32},{32,48},{48,64},{64,80},{80,96},{96,112},{112,128},... | collective-permute-start | bytes 73736 | tf_op jit(solution)/shard_map/ppermute | solution.py:12
  736.0 5.1 collective-permute-start.13
  (2 other events, 1.4 us)
Sparse Core Ops, SparseCore 0:
  27.7 193.7 all-reduce.13
  225.0 144.2 all-gather.2
  508.4 213.2 all-reduce.15
